TPU v7x, 32 devices: a whole 2x2x4 slice. The times are simulated.
32 devices in a mesh: harm: 4 (over z), node: 8 (over y, x, core).
Axes of the slice: x: 2, y: 2, z: 4, core: 2. Of those that a mesh axis runs over, the one named last changes fastest.
Arguments:
- adjoint: bfloat16 [128, 4, 32768], P('harm', None, 'node'), may hold values from -6 to 6
- source: float32 [128, 131072], P(None, ('harm', 'node')), may hold values from -6 to 6
- rad_coeff: bfloat16 [128, 131072], P(None, ('harm', 'node')), may hold values from 0.19921875 to 2
- capacity: float32 [131072], P(('harm', 'node')), may hold values from 0.005 to 0.03
- inv_diag: float32 [131072], P(('harm', 'node')), may hold values from 0.1 to 0.5
- blocks: bfloat16 [1024, 4, 128, 128], P(('harm', 'node')), may hold values from -0.25 to 0.25
- block_cols: int32 [1024, 4], P(('harm', 'node')), may hold values from 0 to 1023, as said below
- zone_of: int32 [131072], P(('harm', 'node')), may hold values from 0 to 1279, as said below
- heater_weight: float32 [131072], P(('harm', 'node')), may hold values from 0.2 to 2
Outputs:
- updated: bfloat16 [128, 4, 32768], P('harm', None, 'node')
- gradient: float32 [1280, 128], P(('harm', 'node'))
Inputs may be any that keep to these rules, and one draw needn't show every extreme that they name: `block_cols`: with d = b // 32 and D = 32: slot 0 of row block b names b itself; slot 1 lies in row blocks max(d - 1, 0) * 32 to (max(d - 1, 0) + 1) * 32 - 1; slot 2 in min(d + 1, D - 1) * 32 to (min(d + 1, D - 1) + 1) * 32 - 1; the other slots in (d - 1) * 32 to (d + 2) * 32 - 1. `zone_of`: node n lies in a zone z with (n // 4096 - 1) * 40 <= z < (n // 4096 + 2) * 40.
All inputs are finite; a program needn't handle non-finite values.
Results may differ from a plain program's by a relative error of at most 0.0035.
Values may be sent and summed in bfloat16 or wider, within the bound.
A program may use at most 64 MiB of HBM per device.

v0:
```python
import math
import jax
import jax.numpy as jnp
from jax import lax
from jax.sharding import PartitionSpec as P

ZONE_DEV = 40


def with_halo(value, sides, width):
    for axis, dim in sides:
        count, length = (lax.axis_size(axis), value.shape[dim])
        up = [(i, (i + 1) % count) for i in range(count - 1)]
        down = [(j, i) for i, j in up]
        last = lax.slice_in_dim(value, length - width, length, axis=dim)
        initial = lax.slice_in_dim(value, 0, width, axis=dim)
        before = lax.ppermute(last, axis, up)
        after = lax.ppermute(initial, axis, down)
        value = jnp.concatenate([before, value, after], axis=dim)
    return value


def passed_along(value, axis, steps):
    count = lax.axis_size(axis)
    initial, last = (max(0, -steps), min(count, count - steps))
    return lax.ppermute(value, axis, [(source, source + steps) for source in range(initial, last)])


def fourier_basis(count):
    sample_index = jnp.arange(count, dtype=jnp.float32)[:, None]
    column_index = jnp.arange(count)[None, :]
    half_count = count // 2
    frequency = jnp.where(
        column_index <= half_count, column_index, column_index - half_count
    ).astype(jnp.float32)
    angle = 2.0 * math.pi * frequency * sample_index / count
    values_table = jnp.where(column_index <= half_count, jnp.cos(angle), jnp.sin(angle))
    scaling = jnp.where(
        (column_index == 0) | (column_index == half_count),
        math.sqrt(1.0 / count),
        math.sqrt(2.0 / count),
    )
    return (values_table * scaling).astype(jnp.bfloat16)


def derivative_term(field):
    half_count = field.shape[0] // 2
    wave_number = jnp.arange(1, half_count, dtype=jnp.float32)[:, None]
    zero_row = jnp.zeros((1, field.shape[1]), jnp.float32)
    upper_rows = wave_number * field[half_count + 1 :]
    lower_rows = -wave_number * field[1:half_count]
    return jnp.concatenate([zero_row, upper_rows, zero_row, lower_rows], axis=0)


def body(
    adjoint, source, rad_coeff, capacity, inv_diag, blocks, block_cols, zone_of, heater_weight
):
    arrived = lax.all_to_all(adjoint, "harm", split_axis=1, concat_axis=0, tiled=True)
    harmonics = arrived.shape[0]
    node_count = arrived.shape[2]
    field = arrived.reshape(harmonics, node_count)
    block_size = blocks.shape[2]
    row_blocks = node_count // block_size
    fourier = fourier_basis(harmonics)
    samples = jnp.dot(fourier, field, preferred_element_type=jnp.float32)
    weighted = (rad_coeff.astype(jnp.float32) * samples).astype(jnp.bfloat16)
    radiative = jnp.dot(fourier.T, weighted, preferred_element_type=jnp.float32)
    rate_term = derivative_term(field.astype(jnp.float32))
    padded = with_halo(field, ((("harm", "node"), 1),), node_count)
    position = lax.axis_index(("harm", "node"))
    local_cols = block_cols - (position - 1) * row_blocks
    extended = padded.reshape(harmonics, 3 * row_blocks, block_size)
    gathered = jnp.take(extended, local_cols, axis=1)
    conduction = jnp.einsum(
        "kbsj,bsij->kbi", gathered, blocks, preferred_element_type=jnp.float32
    ).reshape(harmonics, node_count)
    residual = source - (capacity[None, :] * rate_term + conduction + radiative)
    updated = (field.astype(jnp.float32) + inv_diag[None, :] * residual).astype(jnp.bfloat16)
    returned = lax.all_to_all(
        updated.reshape(harmonics, 1, node_count), "harm", split_axis=0, concat_axis=1, tiled=True
    )
    weighted_terms = (updated.astype(jnp.float32) * heater_weight[None, :]).T
    window_zone = zone_of - (position - 1) * ZONE_DEV
    selector = (window_zone[:, None] == jnp.arange(3 * ZONE_DEV, dtype=jnp.int32)[None, :]).astype(
        jnp.float32
    )
    window_sums = jnp.einsum("nz,nk->zk", selector, weighted_terms, precision=lax.Precision.HIGHEST)
    lower_part = window_sums[:ZONE_DEV]
    middle_part = window_sums[ZONE_DEV : 2 * ZONE_DEV]
    upper_part = window_sums[2 * ZONE_DEV :]
    above_terms = passed_along(lower_part, ("harm", "node"), -1)
    below_terms = passed_along(upper_part, ("harm", "node"), 1)
    gradient = middle_part + above_terms + below_terms
    return (returned, gradient)


def solution(mesh):
    in_specs = (
        P("harm", None, "node"),
        P(None, ("harm", "node")),
        P(None, ("harm", "node")),
        P(("harm", "node")),
        P(("harm", "node")),
        P(("harm", "node"), None, None, None),
        P(("harm", "node"), None),
        P(("harm", "node")),
        P(("harm", "node")),
    )
    out_specs = (P("harm", None, "node"), P(("harm", "node"), None))
    return jax.shard_map(body, mesh=mesh, in_specs=in_specs, out_specs=out_specs, check_vma=False)
```

profile of v0, /device:TPU:4, one launch (start us, length us, event | category | flops | bytes accessed | tf_op | source)
XLA Modules:
  0.0 116.6 jit_solution(15993468261064862405)
XLA Ops:
  0.6 0.0 copy-start.6
  0.6 2.8 %copy.35 = bf16[32,4,4096]{2,0,1:T(8,128)(2,1)} copy(bf16[32,4,4096]{2,1,0:T(4,128)(2,1)} %param.9) | data formatting | bytes 2097152 | tf_op args[0]
  3.4 4.9 %all-to-all-start = ((bf16[32,4,4096]{2,0,1:T(8,128)(2,1)}), bf16[32,4,4096]{2,0,1:T(8,128)(2,1)S(1)}, u32[]{:S(2)}, u32[]{:S(2)}) async-start(bf16[32,4,4096]{2,0,1:T(8,128)(2,1)} %copy.35), calls=%async_computation | async-start | bytes 2097152 | tf_op jit(solution)/shard_map/all_to_all | solution.py:58
  8.3 0.0 copy-done.6
  8.3 0.1 copy.40
  8.4 0.1 reshape.72
  8.5 0.1 copy.36
  8.6 25.4 %all-to-all-done = bf16[32,4,4096]{2,0,1:T(8,128)(2,1)S(1)} async-done(((bf16[32,4,4096]{2,0,1:T(8,128)(2,1)}), bf16[32,4,4096]{2,0,1:T(8,128)(2,1)S(1)}, u32[]{:S(2)}, u32[]{:S(2)}) %all-to-all-start) | async-done | bytes 1048608 | tf_op jit(solution)/shard_map/all_to_all | solution.py:58
  34.0 0.0 copy-start
  34.0 2.0 %collective-permute-start.1 = (bf16[128,4096]{1,0:T(8,128)(2,1)S(1)}, bf16[128,4096]{1,0:T(8,128)(2,1)S(1)}, u32[]{:S(2)}, u32[]{:S(2)}) collective-permute-start(bf16[128,4096]{1,0:T(8,128)(2,1)S(1)} %bitcast.39), channel_id=1, source_target_pairs={{1,0},{2,1},{3,2},{4,3},{5,4},{6,5},{7,6},{8,7},{9,8},{10,9},{11,1... | collective-permute-start | bytes 3145736 | tf_op jit(solution)/shard_map/ppermute | solution.py:18
  36.0 2.3 %collective-permute-start = (bf16[128,4096]{1,0:T(8,128)(2,1)S(1)}, bf16[128,4096]{1,0:T(8,128)(2,1)S(1)}, u32[]{:S(2)}, u32[]{:S(2)}) collective-permute-start(bf16[128,4096]{1,0:T(8,128)(2,1)S(1)} %bitcast.40), channel_id=1, source_target_pairs={{0,1},{1,2},{2,3},{3,4},{4,5},{5,6},{6,7},{7,8},{8,9},{9,10},{10,1... | collective-permute-start | bytes 3145736 | tf_op jit(solution)/shard_map/ppermute | solution.py:17
  38.3 0.3 bitcast_convert_fusion
  38.6 0.2 copy.48
  38.9 0.0 copy-done
  38.9 0.4 copy.38
  39.3 1.6 %slice_multiply_fusion.1 = (f32[63,4096]{1,0:T(8,128)}, f32[63,4096]{1,0:T(8,128)}) fusion(f32[128,4096]{1,0:T(8,128)S(1)} %bitcast_convert_fusion, f32[63]{0:T(128)S(1)} %get-tuple-element.10, f32[63]{0:T(128)S(1)} %get-tuple-element.11), kind=kLoop, calls=%fused_computation.24 | loop fusion | flops 516096 | bytes 4129272 | tf_op jit(solution)/shard_map/mul | solution.py:50
  40.9 15.8 %collective-permute-done.1 = bf16[128,4096]{1,0:T(8,128)(2,1)S(1)} collective-permute-done((bf16[128,4096]{1,0:T(8,128)(2,1)S(1)}, bf16[128,4096]{1,0:T(8,128)(2,1)S(1)}, u32[]{:S(2)}, u32[]{:S(2)}) %collective-permute-start.1) | collective-permute-done | bytes 1048608 | tf_op jit(solution)/shard_map/ppermute | solution.py:18
  56.7 0.3 copy_bitcast_fusion
  57.0 4.3 %collective-permute-done = bf16[128,4096]{1,0:T(8,128)(2,1)S(1)} collective-permute-done((bf16[128,4096]{1,0:T(8,128)(2,1)S(1)}, bf16[128,4096]{1,0:T(8,128)(2,1)S(1)}, u32[]{:S(2)}, u32[]{:S(2)}) %collective-permute-start) | collective-permute-done | bytes 1048608 | tf_op jit(solution)/shard_map/ppermute | solution.py:17
  61.4 0.3 copy_bitcast_fusion.1
  61.6 0.4 pad_maximum_fusion
  62.0 3.0 %gather_fusion = bf16[128,128,128]{2,1,0:T(8,128)(2,1)} fusion(bf16[128,96,128]{2,0,1:T(8,128)(2,1)S(1)} %pad_maximum_fusion, s32[1024]{0:T(1024)S(1)} %pad_clamp_fusion), kind=kCustom, calls=%fused_computation | custom fusion | bytes 8389120 | tf_op jit(solution)/shard_map/jit(_take)/gather | solution.py:73
  65.1 6.2 %fusion.5 = f32[32,128,128,1]{1,2,3,0:T(8,128)} fusion(bf16[32,4,128,128]{3,2,1,0:T(8,128)(2,1)} %param.14, bf16[32,4,128,128]{3,2,1,0:T(8,128)(2,1)} %bitcast.44, pred[32,4]{1,0:T(8,128)(4,1)S(1)} %copy.36), kind=kOutput, calls=%fused_computation.8 | convolution fusion | flops 538968064 | bytes 10485888 | tf_op jit(solution)/shard_map/kbsj,bsij->kbi/dot_general | solution.py:74
  71.3 0.0 copy-start.1
  71.3 0.0 copy-start.3
  71.3 0.0 copy-start.4
  71.3 2.0 %copy.41 = f32[128,4096]{1,0:T(8,128)S(1)} copy(f32[128,4096]{0,1:T(8,128)} %bitcast.47) | data formatting | bytes 4194304 | tf_op jit(solution)/shard_map/reshape | solution.py:76
  73.3 0.0 copy-done.1
  73.3 0.0 copy-done.3
  73.3 0.0 copy-done.4
  73.3 5.2 %fusion.4 = bf16[128,4096]{1,0:T(8,128)(2,1)} fusion(f32[128,4096]{1,0:T(8,128)} %param.10, f32[128,4096]{1,0:T(8,128)S(1)} %copy.41, f32[63,4096]{1,0:T(8,128)} %get-tuple-element.7, f32[1,4096]{1,0:T(1,128)S(1)} %broadcast_in_dim.41, f32[63,4096]{1,0:T(8,128)} %get-tuple-element.6, bf16[128,4096]{1,0:T(8,128)(2,1)S(1)} %bitcast.42, ...), kind=kOutput, calls=%fused_computation.7 | convolution fusion | flops 275939328 | bytes 9454720 | tf_op jit(solution)/shard_map/dot_general | solution.py:67
  78.5 0.5 broadcast.81
  79.0 2.6 %reduce = bf16[128,4096]{1,0:T(8,128)(2,1)S(1)} reduce(bf16[128,1,4096]{2,0,1:T(8,128)(2,1)} %bitcast.46, bf16[]{:T(256)} %broadcast.81), dimensions={1}, to_apply=%copy.42.reduce_sub_computation | reduce | bytes 2097154 | tf_op jit(solution)/shard_map/reshape | solution.py:80
  81.7 0.0 copy-start.5
  81.7 0.0 copy-start.2
  81.7 0.0 copy-start.7
  81.7 2.0 %reshape.81 = bf16[4,2,65536]{2,1,0:T(2,128)(2,1)} reshape(bf16[128,4096]{1,0:T(8,128)(2,1)S(1)} %reduce) | data formatting | bytes 2097152
  83.7 3.5 %all-to-all-start.1 = ((bf16[4,2,65536]{2,1,0:T(2,128)(2,1)}), bf16[4,2,65536]{2,1,0:T(2,128)(2,1)S(1)}, u32[]{:S(2)}, u32[]{:S(2)}) async-start(bf16[4,2,65536]{2,1,0:T(2,128)(2,1)} %reshape.81), calls=%async_computation.1 | async-start | bytes 2097152 | tf_op jit(solution)/shard_map/all_to_all | solution.py:79
  87.2 0.0 copy-done.5
  87.2 0.0 copy-done.2
  87.3 0.0 copy-done.7
  87.3 2.1 %fusion.11 = f32[120,128]{1,0:T(8,128)S(1)} fusion(bf16[128,4096]{1,0:T(8,128)(2,1)S(1)} %copy-done.2, f32[4096]{0:T(1024)S(1)} %copy-done.7, s32[4096]{0:T(1024)S(1)} %broadcast_subtract_fusion), kind=kOutput, calls=%fused_computation.16 | convolution fusion | flops 757006336 | bytes 1142784 | tf_op jit(solution)/shard_map/nz,nk->zk/dot_general | solution.py:87
  89.4 1.9 %collective-permute-start.2 = (f32[40,128]{1,0:T(8,128)S(1)}, f32[40,128]{1,0:T(8,128)S(1)}, u32[]{:S(2)}, u32[]{:S(2)}) collective-permute-start(f32[40,128]{1,0:T(8,128)S(1)} %get-tuple-element.8), channel_id=1, source_target_pairs={{1,0},{2,1},{3,2},{4,3},{5,4},{6,5},{7,6},{8,7},{9,8},{10,9},{11,1... | collective-permute-start | bytes 61448 | tf_op jit(solution)/shard_map/ppermute | solution.py:26
  91.3 2.4 %collective-permute-start.3 = (f32[40,128]{1,0:T(8,128)S(1)}, f32[40,128]{1,0:T(8,128)S(1)}, u32[]{:S(2)}, u32[]{:S(2)}) collective-permute-start(f32[40,128]{1,0:T(8,128)S(1)} %get-tuple-element.9), channel_id=1, source_target_pairs={{0,1},{1,2},{2,3},{3,4},{4,5},{5,6},{6,7},{7,8},{8,9},{9,10},{10,1... | collective-permute-start | bytes 61448 | tf_op jit(solution)/shard_map/ppermute | solution.py:26
  93.7 0.0 collective-permute-done.2
  93.7 3.6 %collective-permute-done.3 = f32[40,128]{1,0:T(8,128)S(1)} collective-permute-done((f32[40,128]{1,0:T(8,128)S(1)}, f32[40,128]{1,0:T(8,128)S(1)}, u32[]{:S(2)}, u32[]{:S(2)}) %collective-permute-start.3) | collective-permute-done | bytes 20512 | tf_op jit(solution)/shard_map/ppermute | solution.py:26
  97.3 0.6 fusion.26
  97.9 14.8 %all-to-all-done.1 = bf16[4,2,65536]{2,1,0:T(2,128)(2,1)S(1)} async-done(((bf16[4,2,65536]{2,1,0:T(2,128)(2,1)}), bf16[4,2,65536]{2,1,0:T(2,128)(2,1)S(1)}, u32[]{:S(2)}, u32[]{:S(2)}) %all-to-all-start.1) | async-done | bytes 1048608 | tf_op jit(solution)/shard_map/all_to_all | solution.py:79
  112.7 0.9 reshape.82
  113.7 1.1 copy.45
  114.9 1.8 %copy.43 = bf16[32,4,4096]{2,1,0:T(4,128)(2,1)} copy(bf16[32,4,4096]{2,0,1:T(8,128)(2,1)S(1)} %bitcast.43) | data formatting | bytes 2097152
  (8 shorter events, 0.1 us)
Async XLA Ops:
  0.6 7.7 %copy-start.6 = (s32[32,4]{0,1:T(4,128)S(1)}, s32[32,4]{0,1:T(4,128)}, u32[]{:S(2)}) copy-start(s32[32,4]{0,1:T(4,128)} %param.15) | copy-start | bytes 1540
  3.4 30.6 %all-to-all-start = ((bf16[32,4,4096]{2,0,1:T(8,128)(2,1)}), bf16[32,4,4096]{2,0,1:T(8,128)(2,1)S(1)}, u32[]{:S(2)}, u32[]{:S(2)}) async-start(bf16[32,4,4096]{2,0,1:T(8,128)(2,1)} %copy.35), calls=%async_computation | async-start | bytes 2097152 | tf_op jit(solution)/shard_map/all_to_all | solution.py:58
  34.0 4.9 %copy-start = (bf16[32,4,4096]{2,0,1:T(8,128)(2,1)}, bf16[32,4,4096]{2,0,1:T(8,128)(2,1)S(1)}, u32[]{:S(2)}) copy-start(bf16[32,4,4096]{2,0,1:T(8,128)(2,1)S(1)} %all-to-all-done) | copy-start | bytes 3145732
  34.0 22.7 %collective-permute-start.1 = (bf16[128,4096]{1,0:T(8,128)(2,1)S(1)}, bf16[128,4096]{1,0:T(8,128)(2,1)S(1)}, u32[]{:S(2)}, u32[]{:S(2)}) collective-permute-start(bf16[128,4096]{1,0:T(8,128)(2,1)S(1)} %bitcast.39), channel_id=1, source_target_pairs={{1,0},{2,1},{3,2},{4,3},{5,4},{6,5},{7,6},{8,7},{9,8},{10,9},{11,1... | collective-permute-start | bytes 3145736 | tf_op jit(solution)/shard_map/ppermute | solution.py:18
  36.0 25.3 %collective-permute-start = (bf16[128,4096]{1,0:T(8,128)(2,1)S(1)}, bf16[128,4096]{1,0:T(8,128)(2,1)S(1)}, u32[]{:S(2)}, u32[]{:S(2)}) collective-permute-start(bf16[128,4096]{1,0:T(8,128)(2,1)S(1)} %bitcast.40), channel_id=1, source_target_pairs={{0,1},{1,2},{2,3},{3,4},{4,5},{5,6},{6,7},{7,8},{8,9},{9,10},{10,1... | collective-permute-start | bytes 3145736 | tf_op jit(solution)/shard_map/ppermute | solution.py:17
  71.3 2.0 %copy-start.1 = (bf16[32,4,4096]{2,0,1:T(8,128)(2,1)S(1)}, bf16[32,4,4096]{2,0,1:T(8,128)(2,1)}, u32[]{:S(2)}) copy-start(bf16[32,4,4096]{2,0,1:T(8,128)(2,1)} %copy-done) | copy-start | bytes 3145732
  71.3 2.0 %copy-start.3 = (f32[4096]{0:T(1024)S(1)}, f32[4096]{0:T(1024)}, u32[]{:S(2)}) copy-start(f32[4096]{0:T(1024)} %param.12) | copy-start | bytes 49156
  71.3 2.1 %copy-start.4 = (f32[4096]{0:T(1024)S(1)}, f32[4096]{0:T(1024)}, u32[]{:S(2)}) copy-start(f32[4096]{0:T(1024)} %param.13) | copy-start | bytes 49156
  81.7 5.6 %copy-start.5 = (s32[4096]{0:T(1024)S(1)}, s32[4096]{0:T(1024)}, u32[]{:S(2)}) copy-start(s32[4096]{0:T(1024)} %param.16) | copy-start | bytes 49156
  81.7 5.6 %copy-start.2 = (bf16[128,4096]{1,0:T(8,128)(2,1)S(1)}, bf16[128,4096]{1,0:T(8,128)(2,1)}, u32[]{:S(2)}) copy-start(bf16[128,4096]{1,0:T(8,128)(2,1)} %fusion.4) | copy-start | bytes 3145732
  81.7 5.6 %copy-start.7 = (f32[4096]{0:T(1024)S(1)}, f32[4096]{0:T(1024)}, u32[]{:S(2)}) copy-start(f32[4096]{0:T(1024)} %param.17) | copy-start | bytes 49156
  83.7 29.0 %all-to-all-start.1 = ((bf16[4,2,65536]{2,1,0:T(2,128)(2,1)}), bf16[4,2,65536]{2,1,0:T(2,128)(2,1)S(1)}, u32[]{:S(2)}, u32[]{:S(2)}) async-start(bf16[4,2,65536]{2,1,0:T(2,128)(2,1)} %reshape.81), calls=%async_computation.1 | async-start | bytes 2097152 | tf_op jit(solution)/shard_map/all_to_all | solution.py:79
  89.4 4.3 %collective-permute-start.2 = (f32[40,128]{1,0:T(8,128)S(1)}, f32[40,128]{1,0:T(8,128)S(1)}, u32[]{:S(2)}, u32[]{:S(2)}) collective-permute-start(f32[40,128]{1,0:T(8,128)S(1)} %get-tuple-element.8), channel_id=1, source_target_pairs={{1,0},{2,1},{3,2},{4,3},{5,4},{6,5},{7,6},{8,7},{9,8},{10,9},{11,1... | collective-permute-start | bytes 61448 | tf_op jit(solution)/shard_map/ppermute | solution.py:26
  91.3 6.0 %collective-permute-start.3 = (f32[40,128]{1,0:T(8,128)S(1)}, f32[40,128]{1,0:T(8,128)S(1)}, u32[]{:S(2)}, u32[]{:S(2)}) collective-permute-start(f32[40,128]{1,0:T(8,128)S(1)} %get-tuple-element.9), channel_id=1, source_target_pairs={{0,1},{1,2},{2,3},{3,4},{4,5},{5,6},{6,7},{7,8},{8,9},{9,10},{10,1... | collective-permute-start | bytes 61448 | tf_op jit(solution)/shard_map/ppermute | solution.py:26
where the time goes:
time: 117 us
  waiting for transfers between devices  63.9 us (55%)
  starting transfers between devices  17 us (15%)
  local copies, waits for them, and re-layouts  15.8 us (14%)
  matrix products  13.5 us (12%)
  other arithmetic  5.56 us (5%)
    all_to_all x1, waiting for transfers between devices, body(): lax.all_to_all(adjoint, 'harm', split_axis=1, concat_axis=0, tiled=True)  25.4 us
    ppermute x1, waiting for transfers between devices, with_halo(): after = lax.ppermute(initial, axis, down)  15.8 us
    all_to_all x1, waiting for transfers between devices, body(): lax.all_to_all(updated.reshape(harmonics, 1, node_count), 'harm', split_a...  14.8 us
    unnamed x22, local copies, waits for them, and re-layouts  8.93 us
    dot_general x1, matrix products, body(): jnp.einsum('kbsj,bsij->kbi', gathered, blocks, preferred_element_type=jnp...  6.17 us
    dot_general x1, matrix products, body(): radiative = jnp.dot(fourier.T, weighted, preferred_element_type=jnp.float32)  5.2 us
    all_to_all x1, starting transfers between devices, body(): lax.all_to_all(adjoint, 'harm', split_axis=1, concat_axis=0, tiled=True)  4.87 us
    ppermute x2, starting transfers between devices, passed_along(): lax.ppermute(value, axis, [(source, source + steps) for source in range(i...  4.33 us
  transfers between devices with their start and end apart: 6, of which 5 were waited for; matrix products, arithmetic and copies ran while one was open for 5% of the time, Pallas kernels for 0%

commit v1 on v0

--- a/solution.py
+++ b/solution.py
@@ -5,6 +5,28 @@
 from jax.sharding import PartitionSpec as P
 
 ZONE_DEV = 40
+
+
+def cut_along(x, dim, size):
+    before, after = (x.shape[:dim], x.shape[dim + 1 :])
+    return jnp.moveaxis(x.reshape(*before, size, -1, *after), dim, 0)
+
+
+def joined_along(blocks, dim):
+    shape = list(blocks.shape[1:])
+    shape[dim] *= blocks.shape[0]
+    return jnp.moveaxis(blocks, 0, dim).reshape(shape)
+
+
+def pairwise_exchange(shard, axis, split_dim, concat_dim):
+    devices, index = (lax.axis_size(axis), lax.axis_index(axis))
+    blocks = cut_along(shard, split_dim, devices)
+    outs = [blocks[index]]
+    for step in range(1, devices):
+        sent = blocks[index ^ step]
+        outs.append(lax.ppermute(sent, axis, [(i, i ^ step) for i in range(devices)]))
+    blocks = jnp.stack(outs)[index ^ jnp.arange(devices)]
+    return joined_along(blocks, concat_dim)
 
 
 def with_halo(value, sides, width):
@@ -55,7 +77,7 @@
 def body(
     adjoint, source, rad_coeff, capacity, inv_diag, blocks, block_cols, zone_of, heater_weight
 ):
-    arrived = lax.all_to_all(adjoint, "harm", split_axis=1, concat_axis=0, tiled=True)
+    arrived = pairwise_exchange(adjoint, "harm", 1, 0)
     harmonics = arrived.shape[0]
     node_count = arrived.shape[2]
     field = arrived.reshape(harmonics, node_count)

time: 117 us -> 117 us (level)
  waiting for transfers between devices: 63.9 us -> 56.9 us
  local copies, waits for them, and re-layouts: 15.8 us -> 19.8 us
  starting transfers between devices: 17 us -> 20.3 us
    all_to_all x1 -> x0, waiting for transfers between devices: 25.4 us -> none  [body(): lax.all_to_all(adjoint, 'harm', split_axis=1, concat_axis=0, tiled=True)]
    ppermute x0 -> x3, waiting for transfers between devices: none -> 17.5 us  [pairwise_exchange(): lax.ppermute(sent, axis, [(i, i ^ step) for i in range(devices)])]
    another operation x0 -> x1, local copies, waits for them, and re-layouts: none -> 5.07 us
    all_to_all x1 -> x0, starting transfers between devices: 4.87 us -> none  [body(): lax.all_to_all(adjoint, 'harm', split_axis=1, concat_axis=0, tiled=True)]
    ppermute x0 -> x3, starting transfers between devices: none -> 4.58 us  [pairwise_exchange(): lax.ppermute(sent, axis, [(i, i ^ step) for i in range(devices)])]
    all_to_all x1, starting transfers between devices: 3.52 us -> 7.02 us  [body(): lax.all_to_all(updated.reshape(harmonics, 1, node_count), 'harm', split_a...]
    unnamed x22 -> x25, local copies, waits for them, and re-layouts: 8.93 us -> 7.32 us
  transfers between devices with their start and end apart: 6 -> 8, of which waited for: 5 -> 6; matrix products, arithmetic and copies ran while one was open for 5% -> 6% of each run, Pallas kernels for 0% -> 0%
where the time goes in v1:
time: 117 us
  waiting for transfers between devices  56.9 us (49%)
  starting transfers between devices  20.3 us (17%)
  local copies, waits for them, and re-layouts  19.8 us (17%)
  matrix products  13.5 us (12%)
  other arithmetic  5.7 us (5%)
    ppermute x3, waiting for transfers between devices, pairwise_exchange(): lax.ppermute(sent, axis, [(i, i ^ step) for i in range(devices)])  17.5 us
    all_to_all x1, waiting for transfers between devices, body(): lax.all_to_all(updated.reshape(harmonics, 1, node_count), 'harm', split_a...  15.7 us
    ppermute x1, waiting for transfers between devices, with_halo(): after = lax.ppermute(initial, axis, down)  15.6 us
    unnamed x25, local copies, waits for them, and re-layouts  7.32 us
    all_to_all x1, starting transfers between devices, body(): lax.all_to_all(updated.reshape(harmonics, 1, node_count), 'harm', split_a...  7.02 us
    dot_general x1, matrix products, body(): jnp.einsum('kbsj,bsij->kbi', gathered, blocks, preferred_element_type=jnp...  6.16 us
    dot_general x1, matrix products, body(): radiative = jnp.dot(fourier.T, weighted, preferred_element_type=jnp.float32)  5.23 us
    another operation x1, local copies, waits for them, and re-layouts  5.07 us
  transfers between devices with their start and end apart: 8, of which 6 were waited for; matrix products, arithmetic and copies ran while one was open for 6% of the time, Pallas kernels for 0%

profile of v1, /device:TPU:4, one launch (start us, length us, event | category | flops | bytes accessed | tf_op | source)
XLA Modules:
  0.0 117.1 jit_solution(4078237222329528995)
XLA Ops:
  0.6 5.1 %constant_dynamic-slice_fusion.3 = (bf16[32,1,4096]{2,1,0:T(2,128)(2,1)S(1)}, bf16[32,1,4096]{2,1,0:T(2,128)(2,1)S(1)}, bf16[32,1,4096]{2,1,0:T(2,128)(2,1)S(1)}, bf16[32,1,4096]{2,1,0:T(2,128)(2,1)S(1)}) fusion(bf16[32,4,4096]{2,1,0:T(4,128)(2,1)} %param.9, s32[]{:T(128)S(6)} %select_n.59, s32[]{:T(128)S(6)} %select_n.61, s32[]{:T(128)S(6)} %select_n.60, ...), kind=kLoop, calls=%fused_computation.47 | loop fusion | bytes 2097168 | tf_op jit(solution)/shard_map/dynamic-slice.4
  5.7 0.0 copy-start.6
  5.7 0.3 copy.66
  6.0 1.6 %collective-permute-start = (bf16[32,1,4096]{2,0,1:T(8,128)(2,1)S(1)}, bf16[32,1,4096]{2,0,1:T(8,128)(2,1)S(1)}, u32[]{:S(2)}, u32[]{:S(2)}) collective-permute-start(bf16[32,1,4096]{2,0,1:T(8,128)(2,1)S(1)} %copy.66), channel_id=1, source_target_pairs={{0,8},{8,0},{16,24},{24,16},{1,9},{9,1},{17,25},{25,17},{2,10},{10... | collective-permute-start | bytes 786440 | tf_op jit(solution)/shard_map/ppermute | solution.py:27
  7.7 0.3 copy.67
  8.0 2.7 %collective-permute-start.1 = (bf16[32,1,4096]{2,0,1:T(8,128)(2,1)S(1)}, bf16[32,1,4096]{2,0,1:T(8,128)(2,1)S(1)}, u32[]{:S(2)}, u32[]{:S(2)}) collective-permute-start(bf16[32,1,4096]{2,0,1:T(8,128)(2,1)S(1)} %copy.67), channel_id=1, source_target_pairs={{0,16},{8,24},{16,0},{24,8},{1,17},{9,25},{17,1},{25,9},{2,18},{10... | collective-permute-start | bytes 786440 | tf_op jit(solution)/shard_map/ppermute | solution.py:27
  10.6 0.3 copy.68
  10.9 0.3 collective-permute-start.2
  11.3 0.0 copy-done.6
  11.3 0.3 copy.75
  11.6 0.1 copy.59
  11.7 0.1 reshape.109
  11.8 0.1 copy.55
  11.9 6.9 %collective-permute-done = bf16[32,1,4096]{2,0,1:T(8,128)(2,1)S(1)} collective-permute-done((bf16[32,1,4096]{2,0,1:T(8,128)(2,1)S(1)}, bf16[32,1,4096]{2,0,1:T(8,128)(2,1)S(1)}, u32[]{:S(2)}, u32[]{:S(2)}) %collective-permute-start) | collective-permute-done | bytes 262176 | tf_op jit(solution)/shard_map/ppermute | solution.py:27
  18.8 10.6 %collective-permute-done.1 = bf16[32,1,4096]{2,0,1:T(8,128)(2,1)S(1)} collective-permute-done((bf16[32,1,4096]{2,0,1:T(8,128)(2,1)S(1)}, bf16[32,1,4096]{2,0,1:T(8,128)(2,1)S(1)}, u32[]{:S(2)}, u32[]{:S(2)}) %collective-permute-start.1) | collective-permute-done | bytes 262176 | tf_op jit(solution)/shard_map/ppermute | solution.py:27
  29.4 0.0 collective-permute-done.2
  29.4 0.1 maximum_bitcast_fusion
  29.5 0.6 gather_fusion
  30.2 0.0 copy-start
  30.2 1.9 %collective-permute-start.4 = (bf16[128,4096]{1,0:T(8,128)(2,1)S(1)}, bf16[128,4096]{1,0:T(8,128)(2,1)S(1)}, u32[]{:S(2)}, u32[]{:S(2)}) collective-permute-start(bf16[128,4096]{1,0:T(8,128)(2,1)S(1)} %bitcast.43), channel_id=1, source_target_pairs={{1,0},{2,1},{3,2},{4,3},{5,4},{6,5},{7,6},{8,7},{9,8},{10,9},{11,1... | collective-permute-start | bytes 3145736 | tf_op jit(solution)/shard_map/ppermute | solution.py:40
  32.1 2.4 %collective-permute-start.3 = (bf16[128,4096]{1,0:T(8,128)(2,1)S(1)}, bf16[128,4096]{1,0:T(8,128)(2,1)S(1)}, u32[]{:S(2)}, u32[]{:S(2)}) collective-permute-start(bf16[128,4096]{1,0:T(8,128)(2,1)S(1)} %bitcast.44), channel_id=1, source_target_pairs={{0,1},{1,2},{2,3},{3,4},{4,5},{5,6},{6,7},{7,8},{8,9},{9,10},{10,1... | collective-permute-start | bytes 3145736 | tf_op jit(solution)/shard_map/ppermute | solution.py:39
  34.5 0.3 bitcast_convert_fusion
  34.8 0.2 copy.71
  35.1 0.0 copy-done
  35.1 0.4 copy.57
  35.5 1.6 %slice_multiply_fusion.1 = (f32[63,4096]{1,0:T(8,128)}, f32[63,4096]{1,0:T(8,128)}) fusion(f32[128,4096]{1,0:T(8,128)S(1)} %bitcast_convert_fusion, f32[63]{0:T(128)S(1)} %get-tuple-element.14, f32[63]{0:T(128)S(1)} %get-tuple-element.15), kind=kLoop, calls=%fused_computation.25 | loop fusion | flops 516096 | bytes 4129272 | tf_op jit(solution)/shard_map/mul | solution.py:72
  37.1 15.6 %collective-permute-done.4 = bf16[128,4096]{1,0:T(8,128)(2,1)S(1)} collective-permute-done((bf16[128,4096]{1,0:T(8,128)(2,1)S(1)}, bf16[128,4096]{1,0:T(8,128)(2,1)S(1)}, u32[]{:S(2)}, u32[]{:S(2)}) %collective-permute-start.4) | collective-permute-done | bytes 1048608 | tf_op jit(solution)/shard_map/ppermute | solution.py:40
  52.7 0.3 copy_bitcast_fusion
  53.0 4.5 %collective-permute-done.3 = bf16[128,4096]{1,0:T(8,128)(2,1)S(1)} collective-permute-done((bf16[128,4096]{1,0:T(8,128)(2,1)S(1)}, bf16[128,4096]{1,0:T(8,128)(2,1)S(1)}, u32[]{:S(2)}, u32[]{:S(2)}) %collective-permute-start.3) | collective-permute-done | bytes 1048608 | tf_op jit(solution)/shard_map/ppermute | solution.py:39
  57.5 0.3 copy_bitcast_fusion.1
  57.8 0.4 pad_maximum_fusion
  58.2 3.0 %gather_fusion.1 = bf16[128,128,128]{2,1,0:T(8,128)(2,1)} fusion(bf16[128,96,128]{2,0,1:T(8,128)(2,1)S(1)} %pad_maximum_fusion, s32[1024]{0:T(1024)S(1)} %pad_clamp_fusion), kind=kCustom, calls=%fused_computation.1 | custom fusion | bytes 8389120 | tf_op jit(solution)/shard_map/jit(_take)/gather | solution.py:95
  61.3 6.2 %fusion.5 = f32[32,128,128,1]{1,2,3,0:T(8,128)} fusion(bf16[32,4,128,128]{3,2,1,0:T(8,128)(2,1)} %param.14, bf16[32,4,128,128]{3,2,1,0:T(8,128)(2,1)} %bitcast.48, pred[32,4]{1,0:T(8,128)(4,1)S(1)} %copy.55), kind=kOutput, calls=%fused_computation.9 | convolution fusion | flops 538968064 | bytes 10485888 | tf_op jit(solution)/shard_map/kbsj,bsij->kbi/dot_general | solution.py:96
  67.4 0.0 copy-start.1
  67.4 0.0 copy-start.3
  67.4 0.0 copy-start.4
  67.4 2.0 %copy.60 = f32[128,4096]{1,0:T(8,128)S(1)} copy(f32[128,4096]{0,1:T(8,128)} %bitcast.51) | data formatting | bytes 4194304 | tf_op jit(solution)/shard_map/reshape | solution.py:98
  69.5 0.0 copy-done.1
  69.5 0.0 copy-done.3
  69.5 0.0 copy-done.4
  69.5 5.2 %fusion.4 = bf16[128,4096]{1,0:T(8,128)(2,1)} fusion(f32[128,4096]{1,0:T(8,128)} %param.10, f32[128,4096]{1,0:T(8,128)S(1)} %copy.60, f32[63,4096]{1,0:T(8,128)} %get-tuple-element.7, f32[1,4096]{1,0:T(1,128)S(1)} %broadcast_in_dim.42, f32[63,4096]{1,0:T(8,128)} %get-tuple-element.6, bf16[128,4096]{1,0:T(8,128)(2,1)S(1)} %bitcast.46, ...), kind=kOutput, calls=%fused_computation.8 | convolution fusion | flops 275939328 | bytes 9454720 | tf_op jit(solution)/shard_map/dot_general | solution.py:89
  74.7 0.5 broadcast.116
  75.2 2.6 %reduce = bf16[128,4096]{1,0:T(8,128)(2,1)S(1)} reduce(bf16[128,1,4096]{2,0,1:T(8,128)(2,1)} %bitcast.50, bf16[]{:T(256)} %broadcast.116), dimensions={1}, to_apply=%copy.61.reduce_sub_computation | reduce | bytes 2097154 | tf_op jit(solution)/shard_map/reshape | solution.py:102
  77.9 0.0 copy-start.5
  77.9 0.0 copy-start.2
  77.9 0.0 copy-start.7
  77.9 2.0 %reshape.120 = bf16[4,2,65536]{2,1,0:T(2,128)(2,1)} reshape(bf16[128,4096]{1,0:T(8,128)(2,1)S(1)} %reduce) | data formatting | bytes 2097152
  79.9 7.0 %all-to-all-start = ((bf16[4,2,65536]{2,1,0:T(2,128)(2,1)}), bf16[4,2,65536]{2,1,0:T(2,128)(2,1)S(1)}, u32[]{:S(2)}, u32[]{:S(2)}) async-start(bf16[4,2,65536]{2,1,0:T(2,128)(2,1)} %reshape.120), calls=%async_computation | async-start | bytes 2097152 | tf_op jit(solution)/shard_map/all_to_all | solution.py:101
  86.9 0.0 copy-done.5
  86.9 0.0 copy-done.2
  86.9 0.0 copy-done.7
  86.9 2.1 %fusion.11 = f32[120,128]{1,0:T(8,128)S(1)} fusion(bf16[128,4096]{1,0:T(8,128)(2,1)S(1)} %copy-done.2, f32[4096]{0:T(1024)S(1)} %copy-done.7, s32[4096]{0:T(1024)S(1)} %broadcast_subtract_fusion), kind=kOutput, calls=%fused_computation.17 | convolution fusion | flops 757006336 | bytes 1142784 | tf_op jit(solution)/shard_map/nz,nk->zk/dot_general | solution.py:109
  89.0 1.9 %collective-permute-start.5 = (f32[40,128]{1,0:T(8,128)S(1)}, f32[40,128]{1,0:T(8,128)S(1)}, u32[]{:S(2)}, u32[]{:S(2)}) collective-permute-start(f32[40,128]{1,0:T(8,128)S(1)} %get-tuple-element.12), channel_id=1, source_target_pairs={{1,0},{2,1},{3,2},{4,3},{5,4},{6,5},{7,6},{8,7},{9,8},{10,9},{11,1... | collective-permute-start | bytes 61448 | tf_op jit(solution)/shard_map/ppermute | solution.py:48
  91.0 2.4 %collective-permute-start.6 = (f32[40,128]{1,0:T(8,128)S(1)}, f32[40,128]{1,0:T(8,128)S(1)}, u32[]{:S(2)}, u32[]{:S(2)}) collective-permute-start(f32[40,128]{1,0:T(8,128)S(1)} %get-tuple-element.13), channel_id=1, source_target_pairs={{0,1},{1,2},{2,3},{3,4},{4,5},{5,6},{6,7},{7,8},{8,9},{9,10},{10,1... | collective-permute-start | bytes 61448 | tf_op jit(solution)/shard_map/ppermute | solution.py:48
  93.4 0.0 collective-permute-done.5
  93.4 3.6 %collective-permute-done.6 = f32[40,128]{1,0:T(8,128)S(1)} collective-permute-done((f32[40,128]{1,0:T(8,128)S(1)}, f32[40,128]{1,0:T(8,128)S(1)}, u32[]{:S(2)}, u32[]{:S(2)}) %collective-permute-start.6) | collective-permute-done | bytes 20512 | tf_op jit(solution)/shard_map/ppermute | solution.py:48
  97.0 0.6 fusion.26
  97.6 15.7 %all-to-all-done = bf16[4,2,65536]{2,1,0:T(2,128)(2,1)S(1)} async-done(((bf16[4,2,65536]{2,1,0:T(2,128)(2,1)}), bf16[4,2,65536]{2,1,0:T(2,128)(2,1)S(1)}, u32[]{:S(2)}, u32[]{:S(2)}) %all-to-all-start) | async-done | bytes 1048608 | tf_op jit(solution)/shard_map/all_to_all | solution.py:101
  113.3 0.9 reshape.121
  114.2 1.1 copy.64
  115.4 1.8 %copy.62 = bf16[32,4,4096]{2,1,0:T(4,128)(2,1)} copy(bf16[32,4,4096]{2,0,1:T(8,128)(2,1)S(1)} %bitcast.47) | data formatting | bytes 2097152
  (10 shorter events, 0.1 us)
Async XLA Ops:
  5.7 5.5 %copy-start.6 = (s32[32,4]{0,1:T(4,128)S(1)}, s32[32,4]{0,1:T(4,128)}, u32[]{:S(2)}) copy-start(s32[32,4]{0,1:T(4,128)} %param.15) | copy-start | bytes 1540
  6.0 12.8 %collective-permute-start = (bf16[32,1,4096]{2,0,1:T(8,128)(2,1)S(1)}, bf16[32,1,4096]{2,0,1:T(8,128)(2,1)S(1)}, u32[]{:S(2)}, u32[]{:S(2)}) collective-permute-start(bf16[32,1,4096]{2,0,1:T(8,128)(2,1)S(1)} %copy.66), channel_id=1, source_target_pairs={{0,8},{8,0},{16,24},{24,16},{1,9},{9,1},{17,25},{25,17},{2,10},{10... | collective-permute-start | bytes 786440 | tf_op jit(solution)/shard_map/ppermute | solution.py:27
  8.0 21.4 %collective-permute-start.1 = (bf16[32,1,4096]{2,0,1:T(8,128)(2,1)S(1)}, bf16[32,1,4096]{2,0,1:T(8,128)(2,1)S(1)}, u32[]{:S(2)}, u32[]{:S(2)}) collective-permute-start(bf16[32,1,4096]{2,0,1:T(8,128)(2,1)S(1)} %copy.67), channel_id=1, source_target_pairs={{0,16},{8,24},{16,0},{24,8},{1,17},{9,25},{17,1},{25,9},{2,18},{10... | collective-permute-start | bytes 786440 | tf_op jit(solution)/shard_map/ppermute | solution.py:27
  10.9 18.5 %collective-permute-start.2 = (bf16[32,1,4096]{2,0,1:T(8,128)(2,1)S(1)}, bf16[32,1,4096]{2,0,1:T(8,128)(2,1)S(1)}, u32[]{:S(2)}, u32[]{:S(2)}) collective-permute-start(bf16[32,1,4096]{2,0,1:T(8,128)(2,1)S(1)} %copy.68), channel_id=1, source_target_pairs={{0,24},{8,16},{16,8},{24,0},{1,25},{9,17},{17,9},{25,1},{2,26},{10... | collective-permute-start | bytes 786440 | tf_op jit(solution)/shard_map/ppermute | solution.py:27
  30.2 4.9 %copy-start = (bf16[4,32,4096]{2,1,0:T(8,128)(2,1)}, bf16[4,32,4096]{2,1,0:T(8,128)(2,1)S(1)}, u32[]{:S(2)}) copy-start(bf16[4,32,4096]{2,1,0:T(8,128)(2,1)S(1)} %gather_fusion) | copy-start | bytes 3145732
  30.2 22.6 %collective-permute-start.4 = (bf16[128,4096]{1,0:T(8,128)(2,1)S(1)}, bf16[128,4096]{1,0:T(8,128)(2,1)S(1)}, u32[]{:S(2)}, u32[]{:S(2)}) collective-permute-start(bf16[128,4096]{1,0:T(8,128)(2,1)S(1)} %bitcast.43), channel_id=1, source_target_pairs={{1,0},{2,1},{3,2},{4,3},{5,4},{6,5},{7,6},{8,7},{9,8},{10,9},{11,1... | collective-permute-start | bytes 3145736 | tf_op jit(solution)/shard_map/ppermute | solution.py:40
  32.1 25.4 %collective-permute-start.3 = (bf16[128,4096]{1,0:T(8,128)(2,1)S(1)}, bf16[128,4096]{1,0:T(8,128)(2,1)S(1)}, u32[]{:S(2)}, u32[]{:S(2)}) collective-permute-start(bf16[128,4096]{1,0:T(8,128)(2,1)S(1)} %bitcast.44), channel_id=1, source_target_pairs={{0,1},{1,2},{2,3},{3,4},{4,5},{5,6},{6,7},{7,8},{8,9},{9,10},{10,1... | collective-permute-start | bytes 3145736 | tf_op jit(solution)/shard_map/ppermute | solution.py:39
  67.4 2.0 %copy-start.1 = (bf16[4,32,4096]{2,1,0:T(8,128)(2,1)S(1)}, bf16[4,32,4096]{2,1,0:T(8,128)(2,1)}, u32[]{:S(2)}) copy-start(bf16[4,32,4096]{2,1,0:T(8,128)(2,1)} %copy-done) | copy-start | bytes 3145732
  67.4 2.0 %copy-start.3 = (f32[4096]{0:T(1024)S(1)}, f32[4096]{0:T(1024)}, u32[]{:S(2)}) copy-start(f32[4096]{0:T(1024)} %param.12) | copy-start | bytes 49156
  67.4 2.1 %copy-start.4 = (f32[4096]{0:T(1024)S(1)}, f32[4096]{0:T(1024)}, u32[]{:S(2)}) copy-start(f32[4096]{0:T(1024)} %param.13) | copy-start | bytes 49156
  77.9 9.0 %copy-start.5 = (s32[4096]{0:T(1024)S(1)}, s32[4096]{0:T(1024)}, u32[]{:S(2)}) copy-start(s32[4096]{0:T(1024)} %param.16) | copy-start | bytes 49156
  77.9 9.0 %copy-start.2 = (bf16[128,4096]{1,0:T(8,128)(2,1)S(1)}, bf16[128,4096]{1,0:T(8,128)(2,1)}, u32[]{:S(2)}) copy-start(bf16[128,4096]{1,0:T(8,128)(2,1)} %fusion.4) | copy-start | bytes 3145732
  77.9 9.0 %copy-start.7 = (f32[4096]{0:T(1024)S(1)}, f32[4096]{0:T(1024)}, u32[]{:S(2)}) copy-start(f32[4096]{0:T(1024)} %param.17) | copy-start | bytes 49156
  79.9 33.4 %all-to-all-start = ((bf16[4,2,65536]{2,1,0:T(2,128)(2,1)}), bf16[4,2,65536]{2,1,0:T(2,128)(2,1)S(1)}, u32[]{:S(2)}, u32[]{:S(2)}) async-start(bf16[4,2,65536]{2,1,0:T(2,128)(2,1)} %reshape.120), calls=%async_computation | async-start | bytes 2097152 | tf_op jit(solution)/shard_map/all_to_all | solution.py:101
  89.0 4.3 %collective-permute-start.5 = (f32[40,128]{1,0:T(8,128)S(1)}, f32[40,128]{1,0:T(8,128)S(1)}, u32[]{:S(2)}, u32[]{:S(2)}) collective-permute-start(f32[40,128]{1,0:T(8,128)S(1)} %get-tuple-element.12), channel_id=1, source_target_pairs={{1,0},{2,1},{3,2},{4,3},{5,4},{6,5},{7,6},{8,7},{9,8},{10,9},{11,1... | collective-permute-start | bytes 61448 | tf_op jit(solution)/shard_map/ppermute | solution.py:48
  91.0 6.0 %collective-permute-start.6 = (f32[40,128]{1,0:T(8,128)S(1)}, f32[40,128]{1,0:T(8,128)S(1)}, u32[]{:S(2)}, u32[]{:S(2)}) collective-permute-start(f32[40,128]{1,0:T(8,128)S(1)} %get-tuple-element.13), channel_id=1, source_target_pairs={{0,1},{1,2},{2,3},{3,4},{4,5},{5,6},{6,7},{7,8},{8,9},{9,10},{10,1... | collective-permute-start | bytes 61448 | tf_op jit(solution)/shard_map/ppermute | solution.py:48
